TPU v7x, 256 devices: a whole 4x4x8 slice. The times are simulated.
256 devices in a mesh: band: 64 (over x, y_hi, z), grid: 4 (over y_lo, core).
Axes of the slice: x: 4, y: 4 (y_hi: 2, y_lo: 2; y = y_hi * 2 + y_lo), z: 8, core: 2. Of those that a mesh axis runs over, the one named last changes fastest.
Arguments:
- bands: float32 [128, 96, 96, 96], P('band', 'grid'), may hold values from -6 to 6
Outputs:
- exchange_out: float32 [128, 96, 96, 96], P('band', 'grid')
All inputs are finite; a program needn't handle non-finite values.
Results may differ from a plain program's by a relative error of at most 0.0091.
Values may be sent and summed in bfloat16 or wider, within the bound.
No kernel may reach another device: no remote copies, remote signals or barrier semaphores. Data moves between devices by JAX's collectives and lax.ppermute only.
A program may use at most 128 MiB of HBM per device.

v0:
```python
import functools

import jax
import jax.numpy as jnp
import numpy as np
from jax import lax
from jax.experimental import pallas as pl
from jax.experimental.pallas import tpu as pltpu
from jax.sharding import PartitionSpec as P


NG = 96
PAIRS = 12
ROWS = 144
THIRD = 48
LANES = 128
SLAB = PAIRS * ROWS
KERNEL_SCALE = 16.0
SCREEN_SQ = 0.05
AXES = ("band", "grid")
BF = jnp.bfloat16
F32 = jnp.float32
BATCH = 6
STEPS = 4
SMALL_VMEM = 24 << 20
WHOLE_VMEM = 58 << 20
LARGE_VMEM = 30 << 20


def dft_table(length):
    half = length // 2
    rows = np.arange(length)
    freq = np.where(rows <= half, rows, rows - half)
    phase = 2.0 * np.pi * np.outer(freq, rows) / length
    return np.where((rows <= half)[:, None], np.cos(phase), np.sin(phase))


def z_tables():
    table = dft_table(NG)
    forward = np.zeros((3, LANES, 2 * LANES))
    inverse = np.zeros((3, 2 * LANES, LANES))
    for g in range(3):
        part = table[:, 32 * g : 32 * g + 32]
        forward[g, :NG, :NG] = table.T
        forward[g, NG:, LANES : LANES + NG] = part.T
        inverse[g, :NG, :NG] = table
        inverse[g, LANES : LANES + NG, NG:] = part
    return jnp.asarray(forward, BF), jnp.asarray(inverse, BF)


def frequency_weights(rows):
    freq = jnp.where(rows <= NG // 2, rows, rows - NG // 2).astype(F32)
    weight = jnp.where((rows == 0) | (rows == NG // 2), 1.0, 2.0) / NG
    return freq * freq, jnp.where(rows < NG, weight, 0.0)


def multiplier_kernel(out):
    dims = (NG, 2 * LANES)
    lane = lax.broadcasted_iota(jnp.int32, dims, 1)
    square_a, weight_a = frequency_weights(lax.broadcasted_iota(jnp.int32, dims, 0))
    square_c, weight_c = frequency_weights(lane % LANES)
    square = square_a + square_c + SCREEN_SQ
    scale = KERNEL_SCALE * weight_a * weight_c
    for q in range(NG // 2):
        even, odd = (frequency_weights(jnp.int32(2 * q + n)) for n in range(2))
        square_b, weight_b = (jnp.where(lane < LANES, *pair) for pair in zip(even, odd))
        out[q * NG : q * NG + NG, :] = scale * weight_b / (square + square_b)


def multiplier():
    return pl.pallas_call(
        multiplier_kernel,
        out_shape=jax.ShapeDtypeStruct((NG // 2 * NG, 2 * LANES), F32),
        compiler_params=pltpu.CompilerParams(vmem_limit_bytes=SMALL_VMEM),
        name="multiplier",
    )()


def dot(left, right):
    return jnp.dot(left, right, preferred_element_type=F32)


def pack_kernel(place, bands, for_a, for_b, b_keep, b_give, c_same, c_other):
    high, core = place[0], place[1]
    mix = high ^ core
    for p in range(bands.shape[1] // 2):
        packed = []
        for band in range(2):
            first, second = bands[band, 2 * p], bands[band, 2 * p + 1]
            heads = (first[:THIRD], first[THIRD:], second[:THIRD])
            rows = [
                jnp.concatenate([heads[g], second[THIRD:, 32 * g : 32 * g + 32]], axis=1)
                for g in range(3)
            ]
            packed.append(jnp.concatenate(rows, axis=0).astype(BF))
            for_a[core ^ band, p] = packed[band]
            for_b[1 - (mix ^ band), p] = packed[band]
        pick = lambda flag: jnp.where(flag == 0, packed[0], packed[1])
        b_keep[p], b_give[p] = pick(mix), pick(1 - mix)
        c_same[p], c_other[p] = pick(high), pick(1 - high)


def one_slab(per):
    return pl.BlockSpec((per, ROWS, LANES), lambda i: (i, 0, 0))


def two_slabs(per):
    return pl.BlockSpec((2, per, ROWS, LANES), lambda i: (0, i, 0, 0))


def shape_of(count):
    dims = (PAIRS, ROWS, LANES)
    return jax.ShapeDtypeStruct(dims if count == 1 else (count, *dims), BF)


def pack(place, bands):
    per = PAIRS // STEPS
    return pl.pallas_call(
        pack_kernel,
        grid=(STEPS,),
        in_specs=[
            pl.BlockSpec(memory_space=pltpu.SMEM),
            pl.BlockSpec((2, 2 * per, NG, NG), lambda i: (0, i, 0, 0)),
        ],
        out_specs=[two_slabs(per)] * 2 + [one_slab(per)] * 4,
        out_shape=[shape_of(2)] * 2 + [shape_of(1)] * 4,
        compiler_params=pltpu.CompilerParams(vmem_limit_bytes=WHOLE_VMEM),
        name="pack",
    )(place, bands)


def unpack_kernel(place, a_same, a_cross, b_cross, b_own, b_mate, c_same, c_cross, out):
    high, core = place[0], place[1]
    mix = high ^ core
    per = out.shape[1] // 2
    start = pl.program_id(0) * per
    for p in range(per):
        load = lambda ref, *at: ref[(*at, start + p)]
        for band in range(2):
            other = core ^ band
            third = jnp.where(mix == band, load(b_own), load(b_mate, 0)).astype(F32)
            fifth = jnp.where(high == band, load(c_same), load(c_cross)).astype(F32)
            total = load(a_same, other).astype(F32) + load(a_cross, other).astype(F32)
            total += third + load(b_cross, 1 - (mix ^ band)).astype(F32)
            total = -(total + fifth)
            out[band, 2 * p] = total[: 2 * THIRD, :NG]
            tail = [total[THIRD * g : THIRD * g + THIRD, NG:] for g in range(3)]
            out[band, 2 * p + 1, :THIRD] = total[2 * THIRD :, :NG]
            out[band, 2 * p + 1, THIRD:] = jnp.concatenate(tail, axis=1)


def unpack(place, *parts):
    per = PAIRS // STEPS
    return pl.pallas_call(
        unpack_kernel,
        grid=(STEPS,),
        in_specs=[pl.BlockSpec(memory_space=pltpu.SMEM)]
        + [pl.BlockSpec(memory_space=pltpu.VMEM)] * len(parts),
        out_specs=pl.BlockSpec((2, 2 * per, NG, NG), lambda i: (0, i, 0, 0)),
        out_shape=jax.ShapeDtypeStruct((2, 2 * PAIRS, NG, NG), F32),
        compiler_params=pltpu.CompilerParams(vmem_limit_bytes=SMALL_VMEM),
        name="unpack",
    )(place, *parts)


def transform(left, right, tables, grid_values, lines, emit):
    y_table, y_back, x_table, x_back, z_table, z_back, weights = tables
    flat = lambda v: v.reshape(-1, v.shape[-1])

    for r in range(4):
        held = lines.at[r % 2]

        def forward_z(i, carry, r=r, held=held):
            part = pl.ds(i * BATCH, BATCH)
            density = left[r][part] * right[r][part]
            sums = [
                dot(flat(density[:, THIRD * g : THIRD * g + THIRD]), z_table[g]) for g in range(3)
            ]
            tail = sums[0][:, LANES:] + sums[1][:, LANES:] + sums[2][:, LANES:]
            keep = lambda v: v.astype(BF).reshape(BATCH, THIRD, LANES)
            held[part, :THIRD, :LANES] = keep(sums[0][:, :LANES])
            held[part, THIRD:, :LANES] = keep(sums[1][:, :LANES])
            held[part, :THIRD, LANES:] = keep(sums[2][:, :LANES])
            held[part, THIRD:, LANES:] = keep(tail)
            return carry

        def forward_y(p, carry, r=r, held=held):
            values = dot(y_table[...], held[p])
            x = r * 2 * PAIRS + 2 * p
            grid_values[pl.ds(x, NG, stride=NG), :] = values[:, :LANES]
            grid_values[pl.ds(x + 1, NG, stride=NG), :] = values[:, LANES:]
            return carry

        lax.fori_loop(0, PAIRS // BATCH, forward_z, 0, unroll=True)
        lax.fori_loop(0, PAIRS, forward_y, 0, unroll=True)

    def middle(q, carry):
        upper = pl.ds(pl.multiple_of(q * 2 * NG, 2 * NG), NG)
        lower = pl.ds(pl.multiple_of(q * 2 * NG + NG, NG), NG)
        block = jnp.concatenate([grid_values[upper, :], grid_values[lower, :]], axis=1).astype(BF)
        scaled = weights[pl.ds(pl.multiple_of(q * NG, NG), NG), :] * dot(x_table[...], block)
        back = dot(x_back[...], scaled.astype(BF))
        grid_values[upper, :] = back[:, :LANES]
        grid_values[lower, :] = back[:, LANES:]
        return carry

    lax.fori_loop(0, NG // 2, middle, 0, unroll=True)

    for r in range(4):
        held = lines.at[r % 2]

        def inverse_y(p, carry, r=r, held=held):
            x = r * 2 * PAIRS + 2 * p
            one = grid_values[pl.ds(x, NG, stride=NG), :]
            two = grid_values[pl.ds(x + 1, NG, stride=NG), :]
            held[p] = dot(y_back[...], jnp.concatenate([one, two], axis=1).astype(BF)).astype(BF)
            return carry

        def inverse_z(i, carry, r=r, held=held):
            part = pl.ds(i * BATCH, BATCH)
            last = flat(held[part, THIRD:, LANES:])
            heads = (
                held[part, :THIRD, :LANES],
                held[part, THIRD:, :LANES],
                held[part, :THIRD, LANES:],
            )
            for g in range(3):
                values = dot(jnp.concatenate([flat(heads[g]), last], axis=1), z_back[g])
                at = (part, slice(THIRD * g, THIRD * g + THIRD))
                emit(r, at, values.astype(BF).reshape(BATCH, THIRD, LANES))
            return carry

        lax.fori_loop(0, PAIRS, inverse_y, 0, unroll=True)
        lax.fori_loop(0, PAIRS // BATCH, inverse_z, 0, unroll=True)


def slabs_of(refs, count):
    parts = [ref if len(ref.shape) == 3 else ref.at[0] for ref in refs[: 4 * count]]
    return [parts[4 * n : 4 * n + 4] for n in range(count)]


def first_kernel(*refs):
    c, b = slabs_of(refs[7:], 2)
    field_cb = refs[15]

    def emit(r, at, potential):
        field_cb[(r, *at)] = potential

    transform(c, b, refs[:7], *refs[16:], emit)


def second_kernel(*refs):
    c, b, a = slabs_of(refs[7:], 3)
    field_cb, field_ca, c_keep, c_give = refs[19:23]
    out = (c_keep.at[0], c_give.at[0], c_keep.at[1], c_give.at[1])

    def emit(r, at, potential):
        field_ca[(r, *at)] = potential
        total = field_cb[(r, *at)].astype(F32) * b[r][at].astype(F32)
        out[r][at] = (total + potential.astype(F32) * a[r][at].astype(F32)).astype(BF)

    transform(c, a, refs[:7], *refs[23:], emit)


def third_kernel(*refs):
    c, b, a = slabs_of(refs[7:], 3)
    field_cb, field_ca, b_own, b_far, b_give, a_own, a_far, a_give = refs[19:27]
    out_b = (b_own, b_give.at[0], b_far, b_give.at[1])
    out_a = (a_own, a_give.at[0], a_far, a_give.at[1])

    def emit(r, at, potential):
        field = potential.astype(F32)
        one, two, three = (v[r][at].astype(F32) for v in (c, b, a))
        out_b[r][at] = (field_cb[(r, *at)].astype(F32) * one + field * three).astype(BF)
        out_a[r][at] = (field_ca[(r, *at)].astype(F32) * one + field * two).astype(BF)

    transform(b, a, refs[:7], *refs[27:], emit)


def call_transform(kernel, name, tables, slabs, outs):
    return pl.pallas_call(
        kernel,
        in_specs=[pl.BlockSpec(memory_space=pltpu.VMEM)] * (len(tables) + len(slabs)),
        out_specs=[pl.BlockSpec(memory_space=pltpu.VMEM)] * len(outs),
        out_shape=[shape_of(count) for count in outs],
        scratch_shapes=[
            pltpu.VMEM((NG * NG, LANES), F32),
            pltpu.VMEM((2, PAIRS, NG, 2 * LANES), BF),
        ],
        compiler_params=pltpu.CompilerParams(vmem_limit_bytes=LARGE_VMEM),
        cost_estimate=pl.CostEstimate(
            flops=1 << 20, bytes_accessed=1 << 16, transcendentals=0
        ),
        name=name,
    )(*tables, *slabs)


def sum_kernel(kept, received, same, cross):
    for n, out in enumerate((same, cross)):
        out[...] = (kept[n].astype(F32) + received[n].astype(F32)).astype(BF)


def add_halves(kept, received):
    return pl.pallas_call(
        sum_kernel,
        out_shape=[shape_of(1)] * 2,
        compiler_params=pltpu.CompilerParams(vmem_limit_bytes=SMALL_VMEM),
        name="add_halves",
    )(kept, received)


def passed(value, blocks, by, length):
    pairs = [
        (4 * k + s, 4 * ((k + by) % length) + (s ^ blocks)) for k in range(length) for s in range(4)
    ]
    return lax.ppermute(value, AXES, pairs)


def per_device(bands):
    length = lax.axis_size("band")
    me = lax.axis_index("grid")
    place = jnp.stack([me // 2, me % 2]).astype(jnp.int32)
    send = functools.partial(passed, length=length)

    table = dft_table(NG)
    orders = [np.concatenate([np.arange(24) + 24 * (r ^ s) for r in range(4)]) for s in range(4)]
    both = np.stack([np.stack([table[:, order], table[:, order].T]) for order in orders])
    x_tables = lax.dynamic_index_in_dim(jnp.asarray(both, BF), me, 0, keepdims=False)

    for_a, for_b, b_keep, b_give, c_same, c_other = pack(place, bands)
    moved = (
        send(c_same, 0, 2),
        send(c_other, 2, 2),
        send(for_b, 2, 0),
        send(for_a, 0, -1),
        send(for_a, 2, -1),
    )
    moved, x_tables = lax.optimization_barrier((moved, x_tables))
    c_same, c_cross, b_cross, a_same, a_cross = moved
    to_mate = lambda value: send(value, 1, 0)
    b = [b_keep, to_mate(b_give), b_cross, to_mate(b_cross[1])]
    a = [a_same, to_mate(a_same[1]), a_cross, to_mate(a_cross[1])]

    c = [c_same, to_mate(c_same), c_cross, to_mate(c_cross)]

    y_table, y_back = jnp.asarray(table, BF), jnp.asarray(table.T, BF)
    tables = (y_table, y_back, x_tables[0], x_tables[1], *z_tables(), multiplier())
    (field_cb,) = call_transform(first_kernel, "pair_cb", tables, [*c, *b], [4])
    field_ca, c_keep, c_give = call_transform(
        second_kernel, "pair_ca", tables, [*c, *b, *a, field_cb], [4, 2, 2]
    )
    sums = add_halves(c_keep, to_mate(c_give))
    c_same, c_cross, field_ca = lax.optimization_barrier((*sums, field_ca))
    c_same, c_cross = send(c_same, 0, -2), send(c_cross, 2, -2)
    b_own, b_far, b_give, a_own, a_far, a_give = call_transform(
        third_kernel, "pair_ba", tables, [*c, *b, *a, field_cb, field_ca], [1, 1, 2, 1, 1, 2]
    )
    a_mate, b_mate = to_mate(a_give), to_mate(b_give)
    a_same = send(jnp.stack([a_own, a_mate[0]]), 0, 1)
    a_cross = send(jnp.stack([a_far, a_mate[1]]), 2, 1)
    b_cross = send(jnp.stack([b_far, b_mate[1]]), 2, 0)
    return unpack(place, a_same, a_cross, b_cross, b_own, b_mate, c_same, c_cross)


def solution(mesh):
    spec = P("band", "grid", None, None)
    return jax.shard_map(
        per_device, mesh=mesh, in_specs=(spec,), out_specs=spec, check_vma=False
    )
```

profile of v0, /device:TPU:32, one launch (start us, length us, event | category | flops | bytes accessed | tf_op | source)
XLA Modules:
  0.0 168.0 jit_solution(15628548614513198506)
XLA Ops:
  0.0 0.6 pad_add_fusion.place
  0.6 4.3 %pack.1 = (bf16[2,12,144,128]{3,2,1,0:T(8,128)(2,1)}, bf16[2,12,144,128]{3,2,1,0:T(8,128)(2,1)}, bf16[12,144,128]{2,1,0:T(8,128)(2,1)}, bf16[12,144,128]{2,1,0:T...) custom-call(s32[2]{0:T(128)} %pad_add_fusion.place, f32[2,24,96,96]{3,2,1,0:T(8,128)} %bands.1), custom_call_target="tpu_custom_call" | custom-call | tf_op jit(solution)/shard_map/pack/pallas_call | solution.py:118
  4.9 1.6 collective-permute-start.2
  6.5 1.7 %collective-permute-start.4 = (bf16[2,12,144,128]{3,2,1,0:T(8,128)(2,1)}, bf16[2,12,144,128]{3,2,1,0:T(8,128)(2,1)S(1)}, u32[]{:S(2)}, u32[]{:S(2)}) collective-permute-start(bf16[2,12,144,128]{3,2,1,0:T(8,128)(2,1)} %get-tuple-element.34), channel_id=1, source_target_pairs={{0,254},{1,255},{2,252},{3,253},{4,2},{5,3},{6,0},{7,1},{8,6},{9,7... | collective-permute-start | bytes 2654216 | tf_op jit(solution)/shard_map/ppermute | solution.py:316
  8.2 8.0 %collective-permute-start.3 = (bf16[2,12,144,128]{3,2,1,0:T(8,128)(2,1)}, bf16[2,12,144,128]{3,2,1,0:T(8,128)(2,1)S(1)}, u32[]{:S(2)}, u32[]{:S(2)}) collective-permute-start(bf16[2,12,144,128]{3,2,1,0:T(8,128)(2,1)} %get-tuple-element.34), channel_id=1, source_target_pairs={{0,252},{1,253},{2,254},{3,255},{4,0},{5,1},{6,2},{7,3},{8,4},{9,5... | collective-permute-start | bytes 2654216 | tf_op jit(solution)/shard_map/ppermute | solution.py:316
  16.3 0.8 dynamic-slice_bitcast_fusion
  17.1 33.7 %collective-permute-done.refs_7_ = bf16[12,144,128]{2,1,0:T(8,128)(2,1)S(1)} collective-permute-done((bf16[12,144,128]{2,1,0:T(8,128)(2,1)}, bf16[12,144,128]{2,1,0:T(8,128)(2,1)S(1)}, u32[]{:S(2)}, u32[]{:S(2)}) %collective-permute-start) | collective-permute-done | bytes 442400 | tf_op jit(solution)/shard_map/ppermute | solution.py:316
  50.8 11.6 %collective-permute-done.1.refs_9_ = bf16[12,144,128]{2,1,0:T(8,128)(2,1)S(1)} collective-permute-done((bf16[12,144,128]{2,1,0:T(8,128)(2,1)}, bf16[12,144,128]{2,1,0:T(8,128)(2,1)S(1)}, u32[]{:S(2)}, u32[]{:S(2)}) %collective-permute-start.1) | collective-permute-done | bytes 442400 | tf_op jit(solution)/shard_map/ppermute | solution.py:316
  62.6 0.5 collective-permute-start.5
  63.3 0.5 collective-permute-start.10
  63.8 0.4 collective-permute-start.9
  64.2 0.3 multiplier.1.refs_6_
  64.6 0.5 collective-permute-done.5.refs_8_
  65.0 0.6 collective-permute-done.6.refs_10_
  65.7 9.5 %pair_cb.1.refs_19_ = bf16[4,12,144,128]{3,2,1,0:T(8,128)(2,1)S(1)} custom-call(bf16[96,96]{1,0:T(8,128)(2,1)S(1)} %copy-done.4, bf16[96,96]{1,0:T(8,128)(2,1)S(1)} %copy-done.3, bf16[96,96]{1,0:T(8,128)(2,1)S(1)} %get-tuple-element.60.refs_2_, bf16[96,96]{1,0:T(8,128)(2,1)S(1)} %get-tuple-element.59.refs_3_, bf16[3,128,256]{2,1,0:T(8,128)(2,1)S(1)} %copy-done.2, ...), custom_call_target="tpu_custom_call" | custom-call | flops 1048576 | bytes 65536 | tf_op jit(solution)/shard_map/pair_cb/pallas_call | solution.py:281
  75.2 22.6 %pair_ca.1 = (bf16[4,12,144,128]{3,2,1,0:T(8,128)(2,1)S(1)}, bf16[2,12,144,128]{3,2,1,0:T(8,128)(2,1)S(1)}, bf16[2,12,144,128]{3,2,1,0:T(8,128)(2,1)S(1)}) custom-call(bf16[96,96]{1,0:T(8,128)(2,1)S(1)} %copy-done.4, bf16[96,96]{1,0:T(8,128)(2,1)S(1)} %copy-done.3, bf16[96,96]{1,0:T(8,128)(2,1)S(1)} %get-tuple-element.60.refs_2_, ...), custom_call_target="tpu_custom_call" | custom-call | flops 1048576 | bytes 65536 | tf_op jit(solution)/shard_map/pair_ca/pallas_call | solution.py:281
  97.8 0.2 collective-permute-start.11
  98.0 2.3 %collective-permute-done.11.received = bf16[2,12,144,128]{3,2,1,0:T(8,128)(2,1)S(1)} collective-permute-done((bf16[2,12,144,128]{3,2,1,0:T(8,128)(2,1)S(1)}, bf16[2,12,144,128]{3,2,1,0:T(8,128)(2,1)S(1)}, u32[]{:S(2)}, u32[]{:S(2)}) %collective-permute-start.11) | collective-permute-done | bytes 884768 | tf_op jit(solution)/shard_map/ppermute | solution.py:316
  100.5 10.2 %pair_ba.1 = (bf16[12,144,128]{2,1,0:T(8,128)(2,1)S(1)}, bf16[12,144,128]{2,1,0:T(8,128)(2,1)S(1)}, bf16[2,12,144,128]{3,2,1,0:T(8,128)(2,1)S(1)}, bf16[12,144,1...) custom-call(bf16[96,96]{1,0:T(8,128)(2,1)S(1)} %copy-done.4, ...), custom_call_target="tpu_custom_call" | custom-call | flops 1048576 | bytes 65536 | tf_op jit(solution)/shard_map/pair_ba/pallas_call | solution.py:281
  110.7 0.2 collective-permute-start.12
  110.9 0.4 collective-permute-start.15
  111.3 1.9 %collective-permute-done.12 = bf16[2,12,144,128]{3,2,1,0:T(8,128)(2,1)S(1)} collective-permute-done((bf16[2,12,144,128]{3,2,1,0:T(8,128)(2,1)S(1)}, bf16[2,12,144,128]{3,2,1,0:T(8,128)(2,1)S(1)}, u32[]{:S(2)}, u32[]{:S(2)}) %collective-permute-start.12) | collective-permute-done | bytes 884768 | tf_op jit(solution)/shard_map/ppermute | solution.py:316
  113.5 0.3 collective-permute-start.14
  113.8 0.6 collective-permute-done.15.b_mate
  114.6 0.2 collective-permute-start.16
  114.8 9.6 %collective-permute-start.17 = (bf16[12,144,128]{2,1,0:T(8,128)(2,1)S(1)}, bf16[12,144,128]{2,1,0:T(8,128)(2,1)S(1)}, u32[]{:S(2)}, u32[]{:S(2)}) collective-permute-start(bf16[12,144,128]{2,1,0:T(8,128)(2,1)S(1)} %get-tuple-element.55), channel_id=1, source_target_pairs={{0,248},{1,249},{2,250},{3,251},{4,252},{5,253},{6,254},{7,255},{8... | collective-permute-start | bytes 1327112 | tf_op jit(solution)/shard_map/ppermute | solution.py:316
  124.4 2.3 %collective-permute-start.18 = (bf16[12,144,128]{2,1,0:T(8,128)(2,1)S(1)}, bf16[12,144,128]{2,1,0:T(8,128)(2,1)S(1)}, u32[]{:S(2)}, u32[]{:S(2)}) collective-permute-start(bf16[12,144,128]{2,1,0:T(8,128)(2,1)S(1)} %get-tuple-element.56), channel_id=1, source_target_pairs={{0,250},{1,251},{2,248},{3,249},{4,254},{5,255},{6,252},{7,253},{8... | collective-permute-start | bytes 1327112 | tf_op jit(solution)/shard_map/ppermute | solution.py:316
  126.8 10.5 %collective-permute-done.17.c_same = bf16[12,144,128]{2,1,0:T(8,128)(2,1)S(1)} collective-permute-done((bf16[12,144,128]{2,1,0:T(8,128)(2,1)S(1)}, bf16[12,144,128]{2,1,0:T(8,128)(2,1)S(1)}, u32[]{:S(2)}, u32[]{:S(2)}) %collective-permute-start.17) | collective-permute-done | bytes 442400 | tf_op jit(solution)/shard_map/ppermute | solution.py:316
  137.2 22.4 %collective-permute-done.18.c_cross = bf16[12,144,128]{2,1,0:T(8,128)(2,1)S(1)} collective-permute-done((bf16[12,144,128]{2,1,0:T(8,128)(2,1)S(1)}, bf16[12,144,128]{2,1,0:T(8,128)(2,1)S(1)}, u32[]{:S(2)}, u32[]{:S(2)}) %collective-permute-start.18) | collective-permute-done | bytes 442400 | tf_op jit(solution)/shard_map/ppermute | solution.py:316
  159.6 1.5 collective-permute-done.14.a_cross
  161.1 3.7 %collective-permute-done.16.b_cross = bf16[2,12,144,128]{3,2,1,0:T(8,128)(2,1)S(1)} collective-permute-done((bf16[2,12,144,128]{3,2,1,0:T(8,128)(2,1)S(1)}, bf16[2,12,144,128]{3,2,1,0:T(8,128)(2,1)S(1)}, u32[]{:S(2)}, u32[]{:S(2)}) %collective-permute-start.16) | collective-permute-done | bytes 884768 | tf_op jit(solution)/shard_map/ppermute | solution.py:316
  164.8 3.0 %unpack.1 = f32[2,24,96,96]{3,2,1,0:T(8,128)} custom-call(s32[2]{0:T(128)S(1)} %copy-done.5, bf16[2,12,144,128]{3,2,1,0:T(8,128)(2,1)S(1)} %collective-permute-done.13.a_same, bf16[2,12,144,128]{3,2,1,0:T(8,128)(2,1)S(1)} %collective-permute-done.14.a_cross, bf16[2,12,144,128]{3,2,1,0:T(8,128)(2,1)S(1)} %collective-permute-done.16.b_cross, ...), custom_call_target="tpu_custom_call" | custom-call | tf_op jit(solution)/shard_map/unpack/pallas_call | solution.py:154
  (36 shorter events, 1.0 us)
Async XLA Ops:
  4.9 57.5 %collective-permute-start.2 = (bf16[2,12,144,128]{3,2,1,0:T(8,128)(2,1)}, bf16[2,12,144,128]{3,2,1,0:T(8,128)(2,1)S(1)}, u32[]{:S(2)}, u32[]{:S(2)}) collective-permute-start(bf16[2,12,144,128]{3,2,1,0:T(8,128)(2,1)} %get-tuple-element.33), channel_id=1, source_target_pairs={{0,2},{1,3},{2,0},{3,1},{4,6},{5,7},{6,4},{7,5},{8,10},{9,11},{10,... | collective-permute-start | bytes 2654216 | tf_op jit(solution)/shard_map/ppermute | solution.py:316
  6.5 55.9 %collective-permute-start.4 = (bf16[2,12,144,128]{3,2,1,0:T(8,128)(2,1)}, bf16[2,12,144,128]{3,2,1,0:T(8,128)(2,1)S(1)}, u32[]{:S(2)}, u32[]{:S(2)}) collective-permute-start(bf16[2,12,144,128]{3,2,1,0:T(8,128)(2,1)} %get-tuple-element.34), channel_id=1, source_target_pairs={{0,254},{1,255},{2,252},{3,253},{4,2},{5,3},{6,0},{7,1},{8,6},{9,7... | collective-permute-start | bytes 2654216 | tf_op jit(solution)/shard_map/ppermute | solution.py:316
  8.2 54.2 %collective-permute-start.3 = (bf16[2,12,144,128]{3,2,1,0:T(8,128)(2,1)}, bf16[2,12,144,128]{3,2,1,0:T(8,128)(2,1)S(1)}, u32[]{:S(2)}, u32[]{:S(2)}) collective-permute-start(bf16[2,12,144,128]{3,2,1,0:T(8,128)(2,1)} %get-tuple-element.34), channel_id=1, source_target_pairs={{0,252},{1,253},{2,254},{3,255},{4,0},{5,1},{6,2},{7,3},{8,4},{9,5... | collective-permute-start | bytes 2654216 | tf_op jit(solution)/shard_map/ppermute | solution.py:316
  16.3 34.5 %collective-permute-start = (bf16[12,144,128]{2,1,0:T(8,128)(2,1)}, bf16[12,144,128]{2,1,0:T(8,128)(2,1)S(1)}, u32[]{:S(2)}, u32[]{:S(2)}) collective-permute-start(bf16[12,144,128]{2,1,0:T(8,128)(2,1)} %get-tuple-element.31), channel_id=1, source_target_pairs={{0,8},{1,9},{2,10},{3,11},{4,12},{5,13},{6,14},{7,15},{8,16},{9,17... | collective-permute-start | bytes 1327112 | tf_op jit(solution)/shard_map/ppermute | solution.py:316
  16.3 46.2 %collective-permute-start.1 = (bf16[12,144,128]{2,1,0:T(8,128)(2,1)}, bf16[12,144,128]{2,1,0:T(8,128)(2,1)S(1)}, u32[]{:S(2)}, u32[]{:S(2)}) collective-permute-start(bf16[12,144,128]{2,1,0:T(8,128)(2,1)} %get-tuple-element.32), channel_id=1, source_target_pairs={{0,10},{1,11},{2,8},{3,9},{4,14},{5,15},{6,12},{7,13},{8,18},{9,19... | collective-permute-start | bytes 1327112 | tf_op jit(solution)/shard_map/ppermute | solution.py:316
  50.8 13.0 %collective-permute-start.7 = (bf16[12,144,128]{2,1,0:T(8,128)(2,1)}, bf16[12,144,128]{2,1,0:T(8,128)(2,1)S(1)}, u32[]{:S(2)}, u32[]{:S(2)}) collective-permute-start(bf16[12,144,128]{2,1,0:T(8,128)(2,1)} %get-tuple-element.39), channel_id=1, source_target_pairs={{0,1},{1,0},{2,3},{3,2},{4,5},{5,4},{6,7},{7,6},{8,9},{9,8},{10,11... | collective-permute-start | bytes 1327112 | tf_op jit(solution)/shard_map/ppermute | solution.py:316
  62.5 2.0 %collective-permute-start.8 = (bf16[12,144,128]{2,1,0:T(8,128)(2,1)S(1)}, bf16[12,144,128]{2,1,0:T(8,128)(2,1)S(1)}, u32[]{:S(2)}, u32[]{:S(2)}) collective-permute-start(bf16[12,144,128]{2,1,0:T(8,128)(2,1)S(1)} %slice_bitcast_fusion.2), channel_id=1, source_target_pairs={{0,1},{1,0},{2,3},{3,2},{4,5},{5,4},{6,7},{7,6},{8,9},{9,8},{10,11... | collective-permute-start | bytes 1327112 | tf_op jit(solution)/shard_map/ppermute | solution.py:316
  62.6 2.4 %collective-permute-start.5 = (bf16[12,144,128]{2,1,0:T(8,128)(2,1)S(1)}, bf16[12,144,128]{2,1,0:T(8,128)(2,1)S(1)}, u32[]{:S(2)}, u32[]{:S(2)}) collective-permute-start(bf16[12,144,128]{2,1,0:T(8,128)(2,1)S(1)} %collective-permute-done.refs_7_), channel_id=1, source_target_pairs={{0,1},{1,0},{2,3},{3,2},{4,5},{5,4},{6,7},{7,6},{8,9},{9,8},{10,11... | collective-permute-start | bytes 1327112 | tf_op jit(solution)/shard_map/ppermute | solution.py:316
  63.1 2.5 %collective-permute-start.6 = (bf16[12,144,128]{2,1,0:T(8,128)(2,1)S(1)}, bf16[12,144,128]{2,1,0:T(8,128)(2,1)S(1)}, u32[]{:S(2)}, u32[]{:S(2)}) collective-permute-start(bf16[12,144,128]{2,1,0:T(8,128)(2,1)S(1)} %collective-permute-done.1.refs_9_), channel_id=1, source_target_pairs={{0,1},{1,0},{2,3},{3,2},{4,5},{5,4},{6,7},{7,6},{8,9},{9,8},{10,11... | collective-permute-start | bytes 1327112 | tf_op jit(solution)/shard_map/ppermute | solution.py:316
  63.3 2.4 %copy-start = (bf16[12,144,128]{2,1,0:T(8,128)(2,1)S(1)}, bf16[12,144,128]{2,1,0:T(8,128)(2,1)}, u32[]{:S(2)}) copy-start(bf16[12,144,128]{2,1,0:T(8,128)(2,1)} %get-tuple-element.38.refs_11_) | copy-start | bytes 1327108
  63.3 2.4 %copy-start.1 = (bf16[3,256,128]{2,1,0:T(8,128)(2,1)S(1)}, bf16[3,256,128]{2,1,0:T(8,128)(2,1)}, u32[]{:S(2)}) copy-start(bf16[3,256,128]{2,1,0:T(8,128)(2,1)} %constant.47.clone.refs_5_) | copy-start | bytes 589828
  63.3 2.4 %copy-start.2 = (bf16[3,128,256]{2,1,0:T(8,128)(2,1)S(1)}, bf16[3,128,256]{2,1,0:T(8,128)(2,1)}, u32[]{:S(2)}) copy-start(bf16[3,128,256]{2,1,0:T(8,128)(2,1)} %constant.46.clone.refs_4_) | copy-start | bytes 589828
  63.3 2.4 %copy-start.3 = (bf16[96,96]{1,0:T(8,128)(2,1)S(1)}, bf16[96,96]{1,0:T(8,128)(2,1)}, u32[]{:S(2)}) copy-start(bf16[96,96]{1,0:T(8,128)(2,1)} %constant.45.clone.refs_1_) | copy-start | bytes 55300
  63.3 2.4 %copy-start.4 = (bf16[96,96]{1,0:T(8,128)(2,1)S(1)}, bf16[96,96]{1,0:T(8,128)(2,1)}, u32[]{:S(2)}) copy-start(bf16[96,96]{1,0:T(8,128)(2,1)} %constant.44.clone.refs_0_) | copy-start | bytes 55300
  63.3 11.8 %collective-permute-start.10 = (bf16[12,144,128]{2,1,0:T(8,128)(2,1)S(1)}, bf16[12,144,128]{2,1,0:T(8,128)(2,1)S(1)}, u32[]{:S(2)}, u32[]{:S(2)}) collective-permute-start(bf16[12,144,128]{2,1,0:T(8,128)(2,1)S(1)} %slice_bitcast_fusion), channel_id=1, source_target_pairs={{0,1},{1,0},{2,3},{3,2},{4,5},{5,4},{6,7},{7,6},{8,9},{9,8},{10,11... | collective-permute-start | bytes 1327112 | tf_op jit(solution)/shard_map/ppermute | solution.py:316
  63.8 11.3 %collective-permute-start.9 = (bf16[12,144,128]{2,1,0:T(8,128)(2,1)S(1)}, bf16[12,144,128]{2,1,0:T(8,128)(2,1)S(1)}, u32[]{:S(2)}, u32[]{:S(2)}) collective-permute-start(bf16[12,144,128]{2,1,0:T(8,128)(2,1)S(1)} %slice_bitcast_fusion.1), channel_id=1, source_target_pairs={{0,1},{1,0},{2,3},{3,2},{4,5},{5,4},{6,7},{7,6},{8,9},{9,8},{10,11... | collective-permute-start | bytes 1327112 | tf_op jit(solution)/shard_map/ppermute | solution.py:316
  97.8 2.5 %collective-permute-start.11 = (bf16[2,12,144,128]{3,2,1,0:T(8,128)(2,1)S(1)}, bf16[2,12,144,128]{3,2,1,0:T(8,128)(2,1)S(1)}, u32[]{:S(2)}, u32[]{:S(2)}) collective-permute-start(bf16[2,12,144,128]{3,2,1,0:T(8,128)(2,1)S(1)} %get-tuple-element.44), channel_id=1, source_target_pairs={{0,1},{1,0},{2,3},{3,2},{4,5},{5,4},{6,7},{7,6},{8,9},{9,8},{10,11... | collective-permute-start | bytes 2654216 | tf_op jit(solution)/shard_map/ppermute | solution.py:316
  110.7 2.5 %collective-permute-start.12 = (bf16[2,12,144,128]{3,2,1,0:T(8,128)(2,1)S(1)}, bf16[2,12,144,128]{3,2,1,0:T(8,128)(2,1)S(1)}, u32[]{:S(2)}, u32[]{:S(2)}) collective-permute-start(bf16[2,12,144,128]{3,2,1,0:T(8,128)(2,1)S(1)} %get-tuple-element.50), channel_id=1, source_target_pairs={{0,1},{1,0},{2,3},{3,2},{4,5},{5,4},{6,7},{7,6},{8,9},{9,8},{10,11... | collective-permute-start | bytes 2654216 | tf_op jit(solution)/shard_map/ppermute | solution.py:316
  110.9 3.6 %collective-permute-start.15 = (bf16[2,12,144,128]{3,2,1,0:T(8,128)(2,1)S(1)}, bf16[2,12,144,128]{3,2,1,0:T(8,128)(2,1)S(1)}, u32[]{:S(2)}, u32[]{:S(2)}) collective-permute-start(bf16[2,12,144,128]{3,2,1,0:T(8,128)(2,1)S(1)} %get-tuple-element.53), channel_id=1, source_target_pairs={{0,1},{1,0},{2,3},{3,2},{4,5},{5,4},{6,7},{7,6},{8,9},{9,8},{10,11... | collective-permute-start | bytes 2654216 | tf_op jit(solution)/shard_map/ppermute | solution.py:316
  113.3 51.5 %copy-start.5 = (s32[2]{0:T(128)S(1)}, s32[2]{0:T(128)}, u32[]{:S(2)}) copy-start(s32[2]{0:T(128)} %pad_add_fusion.place) | copy-start | bytes 28
  113.4 46.3 %collective-permute-start.13 = (bf16[2,12,144,128]{3,2,1,0:T(8,128)(2,1)S(1)}, bf16[2,12,144,128]{3,2,1,0:T(8,128)(2,1)S(1)}, u32[]{:S(2)}, u32[]{:S(2)}) collective-permute-start(bf16[2,12,144,128]{3,2,1,0:T(8,128)(2,1)S(1)} %pad_maximum_fusion), channel_id=1, source_target_pairs={{0,4},{1,5},{2,6},{3,7},{4,8},{5,9},{6,10},{7,11},{8,12},{9,13},{1... | collective-permute-start | bytes 2654216 | tf_op jit(solution)/shard_map/ppermute | solution.py:316
  113.5 47.6 %collective-permute-start.14 = (bf16[2,12,144,128]{3,2,1,0:T(8,128)(2,1)S(1)}, bf16[2,12,144,128]{3,2,1,0:T(8,128)(2,1)S(1)}, u32[]{:S(2)}, u32[]{:S(2)}) collective-permute-start(bf16[2,12,144,128]{3,2,1,0:T(8,128)(2,1)S(1)} %pad_maximum_fusion.1), channel_id=1, source_target_pairs={{0,6},{1,7},{2,4},{3,5},{4,10},{5,11},{6,8},{7,9},{8,14},{9,15},{1... | collective-permute-start | bytes 2654216 | tf_op jit(solution)/shard_map/ppermute | solution.py:316
  114.6 50.2 %collective-permute-start.16 = (bf16[2,12,144,128]{3,2,1,0:T(8,128)(2,1)S(1)}, bf16[2,12,144,128]{3,2,1,0:T(8,128)(2,1)S(1)}, u32[]{:S(2)}, u32[]{:S(2)}) collective-permute-start(bf16[2,12,144,128]{3,2,1,0:T(8,128)(2,1)S(1)} %pad_maximum_fusion.2), channel_id=1, source_target_pairs={{0,2},{1,3},{2,0},{3,1},{4,6},{5,7},{6,4},{7,5},{8,10},{9,11},{10,... | collective-permute-start | bytes 2654216 | tf_op jit(solution)/shard_map/ppermute | solution.py:316
  114.8 22.4 %collective-permute-start.17 = (bf16[12,144,128]{2,1,0:T(8,128)(2,1)S(1)}, bf16[12,144,128]{2,1,0:T(8,128)(2,1)S(1)}, u32[]{:S(2)}, u32[]{:S(2)}) collective-permute-start(bf16[12,144,128]{2,1,0:T(8,128)(2,1)S(1)} %get-tuple-element.55), channel_id=1, source_target_pairs={{0,248},{1,249},{2,250},{3,251},{4,252},{5,253},{6,254},{7,255},{8... | collective-permute-start | bytes 1327112 | tf_op jit(solution)/shard_map/ppermute | solution.py:316
  124.4 35.2 %collective-permute-start.18 = (bf16[12,144,128]{2,1,0:T(8,128)(2,1)S(1)}, bf16[12,144,128]{2,1,0:T(8,128)(2,1)S(1)}, u32[]{:S(2)}, u32[]{:S(2)}) collective-permute-start(bf16[12,144,128]{2,1,0:T(8,128)(2,1)S(1)} %get-tuple-element.56), channel_id=1, source_target_pairs={{0,250},{1,251},{2,248},{3,249},{4,254},{5,255},{6,252},{7,253},{8... | collective-permute-start | bytes 1327112 | tf_op jit(solution)/shard_map/ppermute | solution.py:316
where the time goes:
time: 169 us; the launch traced here: 168 us
  waiting for transfers between devices  89.3 us (53%)
  Pallas kernels  50.1 us (30%)
  starting transfers between devices  26.3 us (16%)
    ppermute x19, waiting for transfers between devices, passed(): return lax.ppermute(value, AXES, pairs)  89.3 us
    pallas_call x3, Pallas kernels, call_transform(): pl.pallas_call(kernel, in_specs=[pl.BlockSpec(memory_space=pltpu.VMEM)] *...  42.2 us
    ppermute x19, starting transfers between devices, passed(): return lax.ppermute(value, AXES, pairs)  26.3 us
    pallas_call x1, Pallas kernels, pack(): pl.pallas_call(pack_kernel, grid=(STEPS,), in_specs=[pl.BlockSpec(memory_...  4.33 us
  transfers between devices with their start and end apart: 19, of which 11 were waited for; matrix products, arithmetic and copies ran while one was open for 1% of the time, Pallas kernels for 6%

commit v1 on v0

--- a/solution.py
+++ b/solution.py
@@ -21,7 +21,7 @@
 BF = jnp.bfloat16
 F32 = jnp.float32
 BATCH = 6
-STEPS = 4
+STEPS = 2
 SMALL_VMEM = 24 << 20
 WHOLE_VMEM = 58 << 20
 LARGE_VMEM = 30 << 20

time: 169 us -> 168 us (level)
  no operation moved by 1% of the time
where the time goes in v1:
time: 168 us; the launch traced here: 167 us
  waiting for transfers between devices  89.3 us (53%)
  Pallas kernels  48.6 us (29%)
  starting transfers between devices  26.3 us (16%)
    ppermute x19, waiting for transfers between devices, passed(): return lax.ppermute(value, AXES, pairs)  89.3 us
    pallas_call x3, Pallas kernels, call_transform(): pl.pallas_call(kernel, in_specs=[pl.BlockSpec(memory_space=pltpu.VMEM)] *...  42.2 us
    ppermute x19, starting transfers between devices, passed(): return lax.ppermute(value, AXES, pairs)  26.3 us
  transfers between devices with their start and end apart: 19, of which 11 were waited for; matrix products, arithmetic and copies ran while one was open for 1% of the time, Pallas kernels for 6%

profile of v1, /device:TPU:32, one launch (start us, length us, event | category | flops | bytes accessed | tf_op | source)
XLA Modules:
  0.0 166.5 jit_solution(17187063271258665455)
XLA Ops:
  0.0 0.6 pad_add_fusion.place
  0.6 3.3 %pack.1 = (bf16[2,12,144,128]{3,2,1,0:T(8,128)(2,1)}, bf16[2,12,144,128]{3,2,1,0:T(8,128)(2,1)}, bf16[12,144,128]{2,1,0:T(8,128)(2,1)}, bf16[12,144,128]{2,1,0:T...) custom-call(s32[2]{0:T(128)} %pad_add_fusion.place, f32[2,24,96,96]{3,2,1,0:T(8,128)} %bands.1), custom_call_target="tpu_custom_call" | custom-call | tf_op jit(solution)/shard_map/pack/pallas_call | solution.py:118
  3.9 1.6 collective-permute-start.2
  5.5 1.7 %collective-permute-start.4 = (bf16[2,12,144,128]{3,2,1,0:T(8,128)(2,1)}, bf16[2,12,144,128]{3,2,1,0:T(8,128)(2,1)S(1)}, u32[]{:S(2)}, u32[]{:S(2)}) collective-permute-start(bf16[2,12,144,128]{3,2,1,0:T(8,128)(2,1)} %get-tuple-element.34), channel_id=1, source_target_pairs={{0,254},{1,255},{2,252},{3,253},{4,2},{5,3},{6,0},{7,1},{8,6},{9,7... | collective-permute-start | bytes 2654216 | tf_op jit(solution)/shard_map/ppermute | solution.py:316
  7.2 8.0 %collective-permute-start.3 = (bf16[2,12,144,128]{3,2,1,0:T(8,128)(2,1)}, bf16[2,12,144,128]{3,2,1,0:T(8,128)(2,1)S(1)}, u32[]{:S(2)}, u32[]{:S(2)}) collective-permute-start(bf16[2,12,144,128]{3,2,1,0:T(8,128)(2,1)} %get-tuple-element.34), channel_id=1, source_target_pairs={{0,252},{1,253},{2,254},{3,255},{4,0},{5,1},{6,2},{7,3},{8,4},{9,5... | collective-permute-start | bytes 2654216 | tf_op jit(solution)/shard_map/ppermute | solution.py:316
  15.3 0.8 dynamic-slice_bitcast_fusion
  16.1 33.7 %collective-permute-done.refs_7_ = bf16[12,144,128]{2,1,0:T(8,128)(2,1)S(1)} collective-permute-done((bf16[12,144,128]{2,1,0:T(8,128)(2,1)}, bf16[12,144,128]{2,1,0:T(8,128)(2,1)S(1)}, u32[]{:S(2)}, u32[]{:S(2)}) %collective-permute-start) | collective-permute-done | bytes 442400 | tf_op jit(solution)/shard_map/ppermute | solution.py:316
  49.8 11.6 %collective-permute-done.1.refs_9_ = bf16[12,144,128]{2,1,0:T(8,128)(2,1)S(1)} collective-permute-done((bf16[12,144,128]{2,1,0:T(8,128)(2,1)}, bf16[12,144,128]{2,1,0:T(8,128)(2,1)S(1)}, u32[]{:S(2)}, u32[]{:S(2)}) %collective-permute-start.1) | collective-permute-done | bytes 442400 | tf_op jit(solution)/shard_map/ppermute | solution.py:316
  61.6 0.5 collective-permute-start.5
  62.3 0.5 collective-permute-start.10
  62.8 0.4 collective-permute-start.9
  63.2 0.3 multiplier.1.refs_6_
  63.6 0.5 collective-permute-done.5.refs_8_
  64.0 0.6 collective-permute-done.6.refs_10_
  64.7 9.5 %pair_cb.1.refs_19_ = bf16[4,12,144,128]{3,2,1,0:T(8,128)(2,1)S(1)} custom-call(bf16[96,96]{1,0:T(8,128)(2,1)S(1)} %copy-done.4, bf16[96,96]{1,0:T(8,128)(2,1)S(1)} %copy-done.3, bf16[96,96]{1,0:T(8,128)(2,1)S(1)} %get-tuple-element.60.refs_2_, bf16[96,96]{1,0:T(8,128)(2,1)S(1)} %get-tuple-element.59.refs_3_, bf16[3,128,256]{2,1,0:T(8,128)(2,1)S(1)} %copy-done.2, ...), custom_call_target="tpu_custom_call" | custom-call | flops 1048576 | bytes 65536 | tf_op jit(solution)/shard_map/pair_cb/pallas_call | solution.py:281
  74.2 22.6 %pair_ca.1 = (bf16[4,12,144,128]{3,2,1,0:T(8,128)(2,1)S(1)}, bf16[2,12,144,128]{3,2,1,0:T(8,128)(2,1)S(1)}, bf16[2,12,144,128]{3,2,1,0:T(8,128)(2,1)S(1)}) custom-call(bf16[96,96]{1,0:T(8,128)(2,1)S(1)} %copy-done.4, bf16[96,96]{1,0:T(8,128)(2,1)S(1)} %copy-done.3, bf16[96,96]{1,0:T(8,128)(2,1)S(1)} %get-tuple-element.60.refs_2_, ...), custom_call_target="tpu_custom_call" | custom-call | flops 1048576 | bytes 65536 | tf_op jit(solution)/shard_map/pair_ca/pallas_call | solution.py:281
  96.8 0.2 collective-permute-start.11
  97.0 2.3 %collective-permute-done.11.received = bf16[2,12,144,128]{3,2,1,0:T(8,128)(2,1)S(1)} collective-permute-done((bf16[2,12,144,128]{3,2,1,0:T(8,128)(2,1)S(1)}, bf16[2,12,144,128]{3,2,1,0:T(8,128)(2,1)S(1)}, u32[]{:S(2)}, u32[]{:S(2)}) %collective-permute-start.11) | collective-permute-done | bytes 884768 | tf_op jit(solution)/shard_map/ppermute | solution.py:316
  99.5 10.2 %pair_ba.1 = (bf16[12,144,128]{2,1,0:T(8,128)(2,1)S(1)}, bf16[12,144,128]{2,1,0:T(8,128)(2,1)S(1)}, bf16[2,12,144,128]{3,2,1,0:T(8,128)(2,1)S(1)}, bf16[12,144,1...) custom-call(bf16[96,96]{1,0:T(8,128)(2,1)S(1)} %copy-done.4, ...), custom_call_target="tpu_custom_call" | custom-call | flops 1048576 | bytes 65536 | tf_op jit(solution)/shard_map/pair_ba/pallas_call | solution.py:281
  109.7 0.2 collective-permute-start.12
  109.9 0.4 collective-permute-start.15
  110.3 1.9 %collective-permute-done.12 = bf16[2,12,144,128]{3,2,1,0:T(8,128)(2,1)S(1)} collective-permute-done((bf16[2,12,144,128]{3,2,1,0:T(8,128)(2,1)S(1)}, bf16[2,12,144,128]{3,2,1,0:T(8,128)(2,1)S(1)}, u32[]{:S(2)}, u32[]{:S(2)}) %collective-permute-start.12) | collective-permute-done | bytes 884768 | tf_op jit(solution)/shard_map/ppermute | solution.py:316
  112.5 0.3 collective-permute-start.14
  112.8 0.6 collective-permute-done.15.b_mate
  113.6 0.2 collective-permute-start.16
  113.8 9.6 %collective-permute-start.17 = (bf16[12,144,128]{2,1,0:T(8,128)(2,1)S(1)}, bf16[12,144,128]{2,1,0:T(8,128)(2,1)S(1)}, u32[]{:S(2)}, u32[]{:S(2)}) collective-permute-start(bf16[12,144,128]{2,1,0:T(8,128)(2,1)S(1)} %get-tuple-element.55), channel_id=1, source_target_pairs={{0,248},{1,249},{2,250},{3,251},{4,252},{5,253},{6,254},{7,255},{8... | collective-permute-start | bytes 1327112 | tf_op jit(solution)/shard_map/ppermute | solution.py:316
  123.4 2.3 %collective-permute-start.18 = (bf16[12,144,128]{2,1,0:T(8,128)(2,1)S(1)}, bf16[12,144,128]{2,1,0:T(8,128)(2,1)S(1)}, u32[]{:S(2)}, u32[]{:S(2)}) collective-permute-start(bf16[12,144,128]{2,1,0:T(8,128)(2,1)S(1)} %get-tuple-element.56), channel_id=1, source_target_pairs={{0,250},{1,251},{2,248},{3,249},{4,254},{5,255},{6,252},{7,253},{8... | collective-permute-start | bytes 1327112 | tf_op jit(solution)/shard_map/ppermute | solution.py:316
  125.7 10.5 %collective-permute-done.17.c_same = bf16[12,144,128]{2,1,0:T(8,128)(2,1)S(1)} collective-permute-done((bf16[12,144,128]{2,1,0:T(8,128)(2,1)S(1)}, bf16[12,144,128]{2,1,0:T(8,128)(2,1)S(1)}, u32[]{:S(2)}, u32[]{:S(2)}) %collective-permute-start.17) | collective-permute-done | bytes 442400 | tf_op jit(solution)/shard_map/ppermute | solution.py:316
  136.2 22.4 %collective-permute-done.18.c_cross = bf16[12,144,128]{2,1,0:T(8,128)(2,1)S(1)} collective-permute-done((bf16[12,144,128]{2,1,0:T(8,128)(2,1)S(1)}, bf16[12,144,128]{2,1,0:T(8,128)(2,1)S(1)}, u32[]{:S(2)}, u32[]{:S(2)}) %collective-permute-start.18) | collective-permute-done | bytes 442400 | tf_op jit(solution)/shard_map/ppermute | solution.py:316
  158.6 1.5 collective-permute-done.14.a_cross
  160.1 3.7 %collective-permute-done.16.b_cross = bf16[2,12,144,128]{3,2,1,0:T(8,128)(2,1)S(1)} collective-permute-done((bf16[2,12,144,128]{3,2,1,0:T(8,128)(2,1)S(1)}, bf16[2,12,144,128]{3,2,1,0:T(8,128)(2,1)S(1)}, u32[]{:S(2)}, u32[]{:S(2)}) %collective-permute-start.16) | collective-permute-done | bytes 884768 | tf_op jit(solution)/shard_map/ppermute | solution.py:316
  163.8 2.5 %unpack.1 = f32[2,24,96,96]{3,2,1,0:T(8,128)} custom-call(s32[2]{0:T(128)S(1)} %copy-done.5, bf16[2,12,144,128]{3,2,1,0:T(8,128)(2,1)S(1)} %collective-permute-done.13.a_same, bf16[2,12,144,128]{3,2,1,0:T(8,128)(2,1)S(1)} %collective-permute-done.14.a_cross, bf16[2,12,144,128]{3,2,1,0:T(8,128)(2,1)S(1)} %collective-permute-done.16.b_cross, ...), custom_call_target="tpu_custom_call" | custom-call | tf_op jit(solution)/shard_map/unpack/pallas_call | solution.py:154
  (36 shorter events, 1.0 us)
Async XLA Ops:
  3.9 57.5 %collective-permute-start.2 = (bf16[2,12,144,128]{3,2,1,0:T(8,128)(2,1)}, bf16[2,12,144,128]{3,2,1,0:T(8,128)(2,1)S(1)}, u32[]{:S(2)}, u32[]{:S(2)}) collective-permute-start(bf16[2,12,144,128]{3,2,1,0:T(8,128)(2,1)} %get-tuple-element.33), channel_id=1, source_target_pairs={{0,2},{1,3},{2,0},{3,1},{4,6},{5,7},{6,4},{7,5},{8,10},{9,11},{10,... | collective-permute-start | bytes 2654216 | tf_op jit(solution)/shard_map/ppermute | solution.py:316
  5.5 55.9 %collective-permute-start.4 = (bf16[2,12,144,128]{3,2,1,0:T(8,128)(2,1)}, bf16[2,12,144,128]{3,2,1,0:T(8,128)(2,1)S(1)}, u32[]{:S(2)}, u32[]{:S(2)}) collective-permute-start(bf16[2,12,144,128]{3,2,1,0:T(8,128)(2,1)} %get-tuple-element.34), channel_id=1, source_target_pairs={{0,254},{1,255},{2,252},{3,253},{4,2},{5,3},{6,0},{7,1},{8,6},{9,7... | collective-permute-start | bytes 2654216 | tf_op jit(solution)/shard_map/ppermute | solution.py:316
  7.2 54.2 %collective-permute-start.3 = (bf16[2,12,144,128]{3,2,1,0:T(8,128)(2,1)}, bf16[2,12,144,128]{3,2,1,0:T(8,128)(2,1)S(1)}, u32[]{:S(2)}, u32[]{:S(2)}) collective-permute-start(bf16[2,12,144,128]{3,2,1,0:T(8,128)(2,1)} %get-tuple-element.34), channel_id=1, source_target_pairs={{0,252},{1,253},{2,254},{3,255},{4,0},{5,1},{6,2},{7,3},{8,4},{9,5... | collective-permute-start | bytes 2654216 | tf_op jit(solution)/shard_map/ppermute | solution.py:316
  15.3 34.5 %collective-permute-start = (bf16[12,144,128]{2,1,0:T(8,128)(2,1)}, bf16[12,144,128]{2,1,0:T(8,128)(2,1)S(1)}, u32[]{:S(2)}, u32[]{:S(2)}) collective-permute-start(bf16[12,144,128]{2,1,0:T(8,128)(2,1)} %get-tuple-element.31), channel_id=1, source_target_pairs={{0,8},{1,9},{2,10},{3,11},{4,12},{5,13},{6,14},{7,15},{8,16},{9,17... | collective-permute-start | bytes 1327112 | tf_op jit(solution)/shard_map/ppermute | solution.py:316
  15.3 46.2 %collective-permute-start.1 = (bf16[12,144,128]{2,1,0:T(8,128)(2,1)}, bf16[12,144,128]{2,1,0:T(8,128)(2,1)S(1)}, u32[]{:S(2)}, u32[]{:S(2)}) collective-permute-start(bf16[12,144,128]{2,1,0:T(8,128)(2,1)} %get-tuple-element.32), channel_id=1, source_target_pairs={{0,10},{1,11},{2,8},{3,9},{4,14},{5,15},{6,12},{7,13},{8,18},{9,19... | collective-permute-start | bytes 1327112 | tf_op jit(solution)/shard_map/ppermute | solution.py:316
  49.8 13.0 %collective-permute-start.7 = (bf16[12,144,128]{2,1,0:T(8,128)(2,1)}, bf16[12,144,128]{2,1,0:T(8,128)(2,1)S(1)}, u32[]{:S(2)}, u32[]{:S(2)}) collective-permute-start(bf16[12,144,128]{2,1,0:T(8,128)(2,1)} %get-tuple-element.39), channel_id=1, source_target_pairs={{0,1},{1,0},{2,3},{3,2},{4,5},{5,4},{6,7},{7,6},{8,9},{9,8},{10,11... | collective-permute-start | bytes 1327112 | tf_op jit(solution)/shard_map/ppermute | solution.py:316
  61.5 2.0 %collective-permute-start.8 = (bf16[12,144,128]{2,1,0:T(8,128)(2,1)S(1)}, bf16[12,144,128]{2,1,0:T(8,128)(2,1)S(1)}, u32[]{:S(2)}, u32[]{:S(2)}) collective-permute-start(bf16[12,144,128]{2,1,0:T(8,128)(2,1)S(1)} %slice_bitcast_fusion.2), channel_id=1, source_target_pairs={{0,1},{1,0},{2,3},{3,2},{4,5},{5,4},{6,7},{7,6},{8,9},{9,8},{10,11... | collective-permute-start | bytes 1327112 | tf_op jit(solution)/shard_map/ppermute | solution.py:316
  61.6 2.4 %collective-permute-start.5 = (bf16[12,144,128]{2,1,0:T(8,128)(2,1)S(1)}, bf16[12,144,128]{2,1,0:T(8,128)(2,1)S(1)}, u32[]{:S(2)}, u32[]{:S(2)}) collective-permute-start(bf16[12,144,128]{2,1,0:T(8,128)(2,1)S(1)} %collective-permute-done.refs_7_), channel_id=1, source_target_pairs={{0,1},{1,0},{2,3},{3,2},{4,5},{5,4},{6,7},{7,6},{8,9},{9,8},{10,11... | collective-permute-start | bytes 1327112 | tf_op jit(solution)/shard_map/ppermute | solution.py:316
  62.1 2.5 %collective-permute-start.6 = (bf16[12,144,128]{2,1,0:T(8,128)(2,1)S(1)}, bf16[12,144,128]{2,1,0:T(8,128)(2,1)S(1)}, u32[]{:S(2)}, u32[]{:S(2)}) collective-permute-start(bf16[12,144,128]{2,1,0:T(8,128)(2,1)S(1)} %collective-permute-done.1.refs_9_), channel_id=1, source_target_pairs={{0,1},{1,0},{2,3},{3,2},{4,5},{5,4},{6,7},{7,6},{8,9},{9,8},{10,11... | collective-permute-start | bytes 1327112 | tf_op jit(solution)/shard_map/ppermute | solution.py:316
  62.3 2.4 %copy-start = (bf16[12,144,128]{2,1,0:T(8,128)(2,1)S(1)}, bf16[12,144,128]{2,1,0:T(8,128)(2,1)}, u32[]{:S(2)}) copy-start(bf16[12,144,128]{2,1,0:T(8,128)(2,1)} %get-tuple-element.38.refs_11_) | copy-start | bytes 1327108
  62.3 2.4 %copy-start.1 = (bf16[3,256,128]{2,1,0:T(8,128)(2,1)S(1)}, bf16[3,256,128]{2,1,0:T(8,128)(2,1)}, u32[]{:S(2)}) copy-start(bf16[3,256,128]{2,1,0:T(8,128)(2,1)} %constant.47.clone.refs_5_) | copy-start | bytes 589828
  62.3 2.4 %copy-start.2 = (bf16[3,128,256]{2,1,0:T(8,128)(2,1)S(1)}, bf16[3,128,256]{2,1,0:T(8,128)(2,1)}, u32[]{:S(2)}) copy-start(bf16[3,128,256]{2,1,0:T(8,128)(2,1)} %constant.46.clone.refs_4_) | copy-start | bytes 589828
  62.3 2.4 %copy-start.3 = (bf16[96,96]{1,0:T(8,128)(2,1)S(1)}, bf16[96,96]{1,0:T(8,128)(2,1)}, u32[]{:S(2)}) copy-start(bf16[96,96]{1,0:T(8,128)(2,1)} %constant.45.clone.refs_1_) | copy-start | bytes 55300
  62.3 2.4 %copy-start.4 = (bf16[96,96]{1,0:T(8,128)(2,1)S(1)}, bf16[96,96]{1,0:T(8,128)(2,1)}, u32[]{:S(2)}) copy-start(bf16[96,96]{1,0:T(8,128)(2,1)} %constant.44.clone.refs_0_) | copy-start | bytes 55300
  62.3 11.8 %collective-permute-start.10 = (bf16[12,144,128]{2,1,0:T(8,128)(2,1)S(1)}, bf16[12,144,128]{2,1,0:T(8,128)(2,1)S(1)}, u32[]{:S(2)}, u32[]{:S(2)}) collective-permute-start(bf16[12,144,128]{2,1,0:T(8,128)(2,1)S(1)} %slice_bitcast_fusion), channel_id=1, source_target_pairs={{0,1},{1,0},{2,3},{3,2},{4,5},{5,4},{6,7},{7,6},{8,9},{9,8},{10,11... | collective-permute-start | bytes 1327112 | tf_op jit(solution)/shard_map/ppermute | solution.py:316
  62.8 11.3 %collective-permute-start.9 = (bf16[12,144,128]{2,1,0:T(8,128)(2,1)S(1)}, bf16[12,144,128]{2,1,0:T(8,128)(2,1)S(1)}, u32[]{:S(2)}, u32[]{:S(2)}) collective-permute-start(bf16[12,144,128]{2,1,0:T(8,128)(2,1)S(1)} %slice_bitcast_fusion.1), channel_id=1, source_target_pairs={{0,1},{1,0},{2,3},{3,2},{4,5},{5,4},{6,7},{7,6},{8,9},{9,8},{10,11... | collective-permute-start | bytes 1327112 | tf_op jit(solution)/shard_map/ppermute | solution.py:316
  96.8 2.5 %collective-permute-start.11 = (bf16[2,12,144,128]{3,2,1,0:T(8,128)(2,1)S(1)}, bf16[2,12,144,128]{3,2,1,0:T(8,128)(2,1)S(1)}, u32[]{:S(2)}, u32[]{:S(2)}) collective-permute-start(bf16[2,12,144,128]{3,2,1,0:T(8,128)(2,1)S(1)} %get-tuple-element.44), channel_id=1, source_target_pairs={{0,1},{1,0},{2,3},{3,2},{4,5},{5,4},{6,7},{7,6},{8,9},{9,8},{10,11... | collective-permute-start | bytes 2654216 | tf_op jit(solution)/shard_map/ppermute | solution.py:316
  109.7 2.5 %collective-permute-start.12 = (bf16[2,12,144,128]{3,2,1,0:T(8,128)(2,1)S(1)}, bf16[2,12,144,128]{3,2,1,0:T(8,128)(2,1)S(1)}, u32[]{:S(2)}, u32[]{:S(2)}) collective-permute-start(bf16[2,12,144,128]{3,2,1,0:T(8,128)(2,1)S(1)} %get-tuple-element.50), channel_id=1, source_target_pairs={{0,1},{1,0},{2,3},{3,2},{4,5},{5,4},{6,7},{7,6},{8,9},{9,8},{10,11... | collective-permute-start | bytes 2654216 | tf_op jit(solution)/shard_map/ppermute | solution.py:316
  109.9 3.6 %collective-permute-start.15 = (bf16[2,12,144,128]{3,2,1,0:T(8,128)(2,1)S(1)}, bf16[2,12,144,128]{3,2,1,0:T(8,128)(2,1)S(1)}, u32[]{:S(2)}, u32[]{:S(2)}) collective-permute-start(bf16[2,12,144,128]{3,2,1,0:T(8,128)(2,1)S(1)} %get-tuple-element.53), channel_id=1, source_target_pairs={{0,1},{1,0},{2,3},{3,2},{4,5},{5,4},{6,7},{7,6},{8,9},{9,8},{10,11... | collective-permute-start | bytes 2654216 | tf_op jit(solution)/shard_map/ppermute | solution.py:316
  112.3 51.5 %copy-start.5 = (s32[2]{0:T(128)S(1)}, s32[2]{0:T(128)}, u32[]{:S(2)}) copy-start(s32[2]{0:T(128)} %pad_add_fusion.place) | copy-start | bytes 28
  112.3 46.3 %collective-permute-start.13 = (bf16[2,12,144,128]{3,2,1,0:T(8,128)(2,1)S(1)}, bf16[2,12,144,128]{3,2,1,0:T(8,128)(2,1)S(1)}, u32[]{:S(2)}, u32[]{:S(2)}) collective-permute-start(bf16[2,12,144,128]{3,2,1,0:T(8,128)(2,1)S(1)} %pad_maximum_fusion), channel_id=1, source_target_pairs={{0,4},{1,5},{2,6},{3,7},{4,8},{5,9},{6,10},{7,11},{8,12},{9,13},{1... | collective-permute-start | bytes 2654216 | tf_op jit(solution)/shard_map/ppermute | solution.py:316
  112.5 47.6 %collective-permute-start.14 = (bf16[2,12,144,128]{3,2,1,0:T(8,128)(2,1)S(1)}, bf16[2,12,144,128]{3,2,1,0:T(8,128)(2,1)S(1)}, u32[]{:S(2)}, u32[]{:S(2)}) collective-permute-start(bf16[2,12,144,128]{3,2,1,0:T(8,128)(2,1)S(1)} %pad_maximum_fusion.1), channel_id=1, source_target_pairs={{0,6},{1,7},{2,4},{3,5},{4,10},{5,11},{6,8},{7,9},{8,14},{9,15},{1... | collective-permute-start | bytes 2654216 | tf_op jit(solution)/shard_map/ppermute | solution.py:316
  113.6 50.2 %collective-permute-start.16 = (bf16[2,12,144,128]{3,2,1,0:T(8,128)(2,1)S(1)}, bf16[2,12,144,128]{3,2,1,0:T(8,128)(2,1)S(1)}, u32[]{:S(2)}, u32[]{:S(2)}) collective-permute-start(bf16[2,12,144,128]{3,2,1,0:T(8,128)(2,1)S(1)} %pad_maximum_fusion.2), channel_id=1, source_target_pairs={{0,2},{1,3},{2,0},{3,1},{4,6},{5,7},{6,4},{7,5},{8,10},{9,11},{10,... | collective-permute-start | bytes 2654216 | tf_op jit(solution)/shard_map/ppermute | solution.py:316
  113.8 22.4 %collective-permute-start.17 = (bf16[12,144,128]{2,1,0:T(8,128)(2,1)S(1)}, bf16[12,144,128]{2,1,0:T(8,128)(2,1)S(1)}, u32[]{:S(2)}, u32[]{:S(2)}) collective-permute-start(bf16[12,144,128]{2,1,0:T(8,128)(2,1)S(1)} %get-tuple-element.55), channel_id=1, source_target_pairs={{0,248},{1,249},{2,250},{3,251},{4,252},{5,253},{6,254},{7,255},{8... | collective-permute-start | bytes 1327112 | tf_op jit(solution)/shard_map/ppermute | solution.py:316
  123.4 35.2 %collective-permute-start.18 = (bf16[12,144,128]{2,1,0:T(8,128)(2,1)S(1)}, bf16[12,144,128]{2,1,0:T(8,128)(2,1)S(1)}, u32[]{:S(2)}, u32[]{:S(2)}) collective-permute-start(bf16[12,144,128]{2,1,0:T(8,128)(2,1)S(1)} %get-tuple-element.56), channel_id=1, source_target_pairs={{0,250},{1,251},{2,248},{3,249},{4,254},{5,255},{6,252},{7,253},{8... | collective-permute-start | bytes 1327112 | tf_op jit(solution)/shard_map/ppermute | solution.py:316

commit v2 on v1

--- a/solution.py
+++ b/solution.py
@@ -20,7 +20,7 @@
 AXES = ("band", "grid")
 BF = jnp.bfloat16
 F32 = jnp.float32
-BATCH = 6
+BATCH = 12
 STEPS = 2
 SMALL_VMEM = 24 << 20
 WHOLE_VMEM = 58 << 20

time: 168 us -> 168 us (level)
  no operation moved by 1% of the time
where the time goes in v2:
time: 168 us; the launch traced here: 167 us
  waiting for transfers between devices  89.3 us (53%)
  Pallas kernels  48.7 us (29%)
  starting transfers between devices  26.3 us (16%)
    ppermute x19, waiting for transfers between devices, passed(): return lax.ppermute(value, AXES, pairs)  89.3 us
    pallas_call x3, Pallas kernels, call_transform(): pl.pallas_call(kernel, in_specs=[pl.BlockSpec(memory_space=pltpu.VMEM)] *...  42.3 us
    ppermute x19, starting transfers between devices, passed(): return lax.ppermute(value, AXES, pairs)  26.3 us
  transfers between devices with their start and end apart: 19, of which 11 were waited for; matrix products, arithmetic and copies ran while one was open for 1% of the time, Pallas kernels for 6%

profile of v2, /device:TPU:32, one launch (start us, length us, event | category | flops | bytes accessed | tf_op | source)
XLA Modules:
  0.0 166.6 jit_solution(14044901708861180960)
XLA Ops:
  0.0 0.6 pad_add_fusion.place
  0.6 3.3 %pack.1 = (bf16[2,12,144,128]{3,2,1,0:T(8,128)(2,1)}, bf16[2,12,144,128]{3,2,1,0:T(8,128)(2,1)}, bf16[12,144,128]{2,1,0:T(8,128)(2,1)}, bf16[12,144,128]{2,1,0:T...) custom-call(s32[2]{0:T(128)} %pad_add_fusion.place, f32[2,24,96,96]{3,2,1,0:T(8,128)} %bands.1), custom_call_target="tpu_custom_call" | custom-call | tf_op jit(solution)/shard_map/pack/pallas_call | solution.py:118
  3.9 1.6 collective-permute-start.2
  5.5 1.7 %collective-permute-start.4 = (bf16[2,12,144,128]{3,2,1,0:T(8,128)(2,1)}, bf16[2,12,144,128]{3,2,1,0:T(8,128)(2,1)S(1)}, u32[]{:S(2)}, u32[]{:S(2)}) collective-permute-start(bf16[2,12,144,128]{3,2,1,0:T(8,128)(2,1)} %get-tuple-element.34), channel_id=1, source_target_pairs={{0,254},{1,255},{2,252},{3,253},{4,2},{5,3},{6,0},{7,1},{8,6},{9,7... | collective-permute-start | bytes 2654216 | tf_op jit(solution)/shard_map/ppermute | solution.py:316
  7.2 8.0 %collective-permute-start.3 = (bf16[2,12,144,128]{3,2,1,0:T(8,128)(2,1)}, bf16[2,12,144,128]{3,2,1,0:T(8,128)(2,1)S(1)}, u32[]{:S(2)}, u32[]{:S(2)}) collective-permute-start(bf16[2,12,144,128]{3,2,1,0:T(8,128)(2,1)} %get-tuple-element.34), channel_id=1, source_target_pairs={{0,252},{1,253},{2,254},{3,255},{4,0},{5,1},{6,2},{7,3},{8,4},{9,5... | collective-permute-start | bytes 2654216 | tf_op jit(solution)/shard_map/ppermute | solution.py:316
  15.3 0.8 dynamic-slice_bitcast_fusion
  16.1 33.7 %collective-permute-done.refs_7_ = bf16[12,144,128]{2,1,0:T(8,128)(2,1)S(1)} collective-permute-done((bf16[12,144,128]{2,1,0:T(8,128)(2,1)}, bf16[12,144,128]{2,1,0:T(8,128)(2,1)S(1)}, u32[]{:S(2)}, u32[]{:S(2)}) %collective-permute-start) | collective-permute-done | bytes 442400 | tf_op jit(solution)/shard_map/ppermute | solution.py:316
  49.8 11.6 %collective-permute-done.1.refs_9_ = bf16[12,144,128]{2,1,0:T(8,128)(2,1)S(1)} collective-permute-done((bf16[12,144,128]{2,1,0:T(8,128)(2,1)}, bf16[12,144,128]{2,1,0:T(8,128)(2,1)S(1)}, u32[]{:S(2)}, u32[]{:S(2)}) %collective-permute-start.1) | collective-permute-done | bytes 442400 | tf_op jit(solution)/shard_map/ppermute | solution.py:316
  61.6 0.5 collective-permute-start.5
  62.3 0.5 collective-permute-start.10
  62.8 0.4 collective-permute-start.9
  63.2 0.3 multiplier.1.refs_6_
  63.6 0.5 collective-permute-done.5.refs_8_
  64.0 0.6 collective-permute-done.6.refs_10_
  64.7 9.6 %pair_cb.1.refs_19_ = bf16[4,12,144,128]{3,2,1,0:T(8,128)(2,1)S(1)} custom-call(bf16[96,96]{1,0:T(8,128)(2,1)S(1)} %copy-done.4, bf16[96,96]{1,0:T(8,128)(2,1)S(1)} %copy-done.3, bf16[96,96]{1,0:T(8,128)(2,1)S(1)} %get-tuple-element.60.refs_2_, bf16[96,96]{1,0:T(8,128)(2,1)S(1)} %get-tuple-element.59.refs_3_, bf16[3,128,256]{2,1,0:T(8,128)(2,1)S(1)} %copy-done.2, ...), custom_call_target="tpu_custom_call" | custom-call | flops 1048576 | bytes 65536 | tf_op jit(solution)/shard_map/pair_cb/pallas_call | solution.py:281
  74.3 22.7 %pair_ca.1 = (bf16[4,12,144,128]{3,2,1,0:T(8,128)(2,1)S(1)}, bf16[2,12,144,128]{3,2,1,0:T(8,128)(2,1)S(1)}, bf16[2,12,144,128]{3,2,1,0:T(8,128)(2,1)S(1)}) custom-call(bf16[96,96]{1,0:T(8,128)(2,1)S(1)} %copy-done.4, bf16[96,96]{1,0:T(8,128)(2,1)S(1)} %copy-done.3, bf16[96,96]{1,0:T(8,128)(2,1)S(1)} %get-tuple-element.60.refs_2_, ...), custom_call_target="tpu_custom_call" | custom-call | flops 1048576 | bytes 65536 | tf_op jit(solution)/shard_map/pair_ca/pallas_call | solution.py:281
  96.9 0.2 collective-permute-start.11
  97.2 2.3 %collective-permute-done.11.received = bf16[2,12,144,128]{3,2,1,0:T(8,128)(2,1)S(1)} collective-permute-done((bf16[2,12,144,128]{3,2,1,0:T(8,128)(2,1)S(1)}, bf16[2,12,144,128]{3,2,1,0:T(8,128)(2,1)S(1)}, u32[]{:S(2)}, u32[]{:S(2)}) %collective-permute-start.11) | collective-permute-done | bytes 884768 | tf_op jit(solution)/shard_map/ppermute | solution.py:316
  99.7 10.1 %pair_ba.1 = (bf16[12,144,128]{2,1,0:T(8,128)(2,1)S(1)}, bf16[12,144,128]{2,1,0:T(8,128)(2,1)S(1)}, bf16[2,12,144,128]{3,2,1,0:T(8,128)(2,1)S(1)}, bf16[12,144,1...) custom-call(bf16[96,96]{1,0:T(8,128)(2,1)S(1)} %copy-done.4, ...), custom_call_target="tpu_custom_call" | custom-call | flops 1048576 | bytes 65536 | tf_op jit(solution)/shard_map/pair_ba/pallas_call | solution.py:281
  109.8 0.2 collective-permute-start.12
  110.0 0.4 collective-permute-start.15
  110.4 1.9 %collective-permute-done.12 = bf16[2,12,144,128]{3,2,1,0:T(8,128)(2,1)S(1)} collective-permute-done((bf16[2,12,144,128]{3,2,1,0:T(8,128)(2,1)S(1)}, bf16[2,12,144,128]{3,2,1,0:T(8,128)(2,1)S(1)}, u32[]{:S(2)}, u32[]{:S(2)}) %collective-permute-start.12) | collective-permute-done | bytes 884768 | tf_op jit(solution)/shard_map/ppermute | solution.py:316
  112.6 0.3 collective-permute-start.14
  112.9 0.6 collective-permute-done.15.b_mate
  113.7 0.2 collective-permute-start.16
  113.9 9.6 %collective-permute-start.17 = (bf16[12,144,128]{2,1,0:T(8,128)(2,1)S(1)}, bf16[12,144,128]{2,1,0:T(8,128)(2,1)S(1)}, u32[]{:S(2)}, u32[]{:S(2)}) collective-permute-start(bf16[12,144,128]{2,1,0:T(8,128)(2,1)S(1)} %get-tuple-element.55), channel_id=1, source_target_pairs={{0,248},{1,249},{2,250},{3,251},{4,252},{5,253},{6,254},{7,255},{8... | collective-permute-start | bytes 1327112 | tf_op jit(solution)/shard_map/ppermute | solution.py:316
  123.5 2.3 %collective-permute-start.18 = (bf16[12,144,128]{2,1,0:T(8,128)(2,1)S(1)}, bf16[12,144,128]{2,1,0:T(8,128)(2,1)S(1)}, u32[]{:S(2)}, u32[]{:S(2)}) collective-permute-start(bf16[12,144,128]{2,1,0:T(8,128)(2,1)S(1)} %get-tuple-element.56), channel_id=1, source_target_pairs={{0,250},{1,251},{2,248},{3,249},{4,254},{5,255},{6,252},{7,253},{8... | collective-permute-start | bytes 1327112 | tf_op jit(solution)/shard_map/ppermute | solution.py:316
  125.8 10.5 %collective-permute-done.17.c_same = bf16[12,144,128]{2,1,0:T(8,128)(2,1)S(1)} collective-permute-done((bf16[12,144,128]{2,1,0:T(8,128)(2,1)S(1)}, bf16[12,144,128]{2,1,0:T(8,128)(2,1)S(1)}, u32[]{:S(2)}, u32[]{:S(2)}) %collective-permute-start.17) | collective-permute-done | bytes 442400 | tf_op jit(solution)/shard_map/ppermute | solution.py:316
  136.3 22.4 %collective-permute-done.18.c_cross = bf16[12,144,128]{2,1,0:T(8,128)(2,1)S(1)} collective-permute-done((bf16[12,144,128]{2,1,0:T(8,128)(2,1)S(1)}, bf16[12,144,128]{2,1,0:T(8,128)(2,1)S(1)}, u32[]{:S(2)}, u32[]{:S(2)}) %collective-permute-start.18) | collective-permute-done | bytes 442400 | tf_op jit(solution)/shard_map/ppermute | solution.py:316
  158.7 1.5 collective-permute-done.14.a_cross
  160.2 3.7 %collective-permute-done.16.b_cross = bf16[2,12,144,128]{3,2,1,0:T(8,128)(2,1)S(1)} collective-permute-done((bf16[2,12,144,128]{3,2,1,0:T(8,128)(2,1)S(1)}, bf16[2,12,144,128]{3,2,1,0:T(8,128)(2,1)S(1)}, u32[]{:S(2)}, u32[]{:S(2)}) %collective-permute-start.16) | collective-permute-done | bytes 884768 | tf_op jit(solution)/shard_map/ppermute | solution.py:316
  163.9 2.5 %unpack.1 = f32[2,24,96,96]{3,2,1,0:T(8,128)} custom-call(s32[2]{0:T(128)S(1)} %copy-done.5, bf16[2,12,144,128]{3,2,1,0:T(8,128)(2,1)S(1)} %collective-permute-done.13.a_same, bf16[2,12,144,128]{3,2,1,0:T(8,128)(2,1)S(1)} %collective-permute-done.14.a_cross, bf16[2,12,144,128]{3,2,1,0:T(8,128)(2,1)S(1)} %collective-permute-done.16.b_cross, ...), custom_call_target="tpu_custom_call" | custom-call | tf_op jit(solution)/shard_map/unpack/pallas_call | solution.py:154
  (36 shorter events, 1.0 us)
Async XLA Ops:
  3.9 57.5 %collective-permute-start.2 = (bf16[2,12,144,128]{3,2,1,0:T(8,128)(2,1)}, bf16[2,12,144,128]{3,2,1,0:T(8,128)(2,1)S(1)}, u32[]{:S(2)}, u32[]{:S(2)}) collective-permute-start(bf16[2,12,144,128]{3,2,1,0:T(8,128)(2,1)} %get-tuple-element.33), channel_id=1, source_target_pairs={{0,2},{1,3},{2,0},{3,1},{4,6},{5,7},{6,4},{7,5},{8,10},{9,11},{10,... | collective-permute-start | bytes 2654216 | tf_op jit(solution)/shard_map/ppermute | solution.py:316
  5.5 55.9 %collective-permute-start.4 = (bf16[2,12,144,128]{3,2,1,0:T(8,128)(2,1)}, bf16[2,12,144,128]{3,2,1,0:T(8,128)(2,1)S(1)}, u32[]{:S(2)}, u32[]{:S(2)}) collective-permute-start(bf16[2,12,144,128]{3,2,1,0:T(8,128)(2,1)} %get-tuple-element.34), channel_id=1, source_target_pairs={{0,254},{1,255},{2,252},{3,253},{4,2},{5,3},{6,0},{7,1},{8,6},{9,7... | collective-permute-start | bytes 2654216 | tf_op jit(solution)/shard_map/ppermute | solution.py:316
  7.2 54.2 %collective-permute-start.3 = (bf16[2,12,144,128]{3,2,1,0:T(8,128)(2,1)}, bf16[2,12,144,128]{3,2,1,0:T(8,128)(2,1)S(1)}, u32[]{:S(2)}, u32[]{:S(2)}) collective-permute-start(bf16[2,12,144,128]{3,2,1,0:T(8,128)(2,1)} %get-tuple-element.34), channel_id=1, source_target_pairs={{0,252},{1,253},{2,254},{3,255},{4,0},{5,1},{6,2},{7,3},{8,4},{9,5... | collective-permute-start | bytes 2654216 | tf_op jit(solution)/shard_map/ppermute | solution.py:316
  15.3 34.5 %collective-permute-start = (bf16[12,144,128]{2,1,0:T(8,128)(2,1)}, bf16[12,144,128]{2,1,0:T(8,128)(2,1)S(1)}, u32[]{:S(2)}, u32[]{:S(2)}) collective-permute-start(bf16[12,144,128]{2,1,0:T(8,128)(2,1)} %get-tuple-element.31), channel_id=1, source_target_pairs={{0,8},{1,9},{2,10},{3,11},{4,12},{5,13},{6,14},{7,15},{8,16},{9,17... | collective-permute-start | bytes 1327112 | tf_op jit(solution)/shard_map/ppermute | solution.py:316
  15.3 46.2 %collective-permute-start.1 = (bf16[12,144,128]{2,1,0:T(8,128)(2,1)}, bf16[12,144,128]{2,1,0:T(8,128)(2,1)S(1)}, u32[]{:S(2)}, u32[]{:S(2)}) collective-permute-start(bf16[12,144,128]{2,1,0:T(8,128)(2,1)} %get-tuple-element.32), channel_id=1, source_target_pairs={{0,10},{1,11},{2,8},{3,9},{4,14},{5,15},{6,12},{7,13},{8,18},{9,19... | collective-permute-start | bytes 1327112 | tf_op jit(solution)/shard_map/ppermute | solution.py:316
  49.8 13.0 %collective-permute-start.7 = (bf16[12,144,128]{2,1,0:T(8,128)(2,1)}, bf16[12,144,128]{2,1,0:T(8,128)(2,1)S(1)}, u32[]{:S(2)}, u32[]{:S(2)}) collective-permute-start(bf16[12,144,128]{2,1,0:T(8,128)(2,1)} %get-tuple-element.39), channel_id=1, source_target_pairs={{0,1},{1,0},{2,3},{3,2},{4,5},{5,4},{6,7},{7,6},{8,9},{9,8},{10,11... | collective-permute-start | bytes 1327112 | tf_op jit(solution)/shard_map/ppermute | solution.py:316
  61.5 2.0 %collective-permute-start.8 = (bf16[12,144,128]{2,1,0:T(8,128)(2,1)S(1)}, bf16[12,144,128]{2,1,0:T(8,128)(2,1)S(1)}, u32[]{:S(2)}, u32[]{:S(2)}) collective-permute-start(bf16[12,144,128]{2,1,0:T(8,128)(2,1)S(1)} %slice_bitcast_fusion.2), channel_id=1, source_target_pairs={{0,1},{1,0},{2,3},{3,2},{4,5},{5,4},{6,7},{7,6},{8,9},{9,8},{10,11... | collective-permute-start | bytes 1327112 | tf_op jit(solution)/shard_map/ppermute | solution.py:316
  61.6 2.4 %collective-permute-start.5 = (bf16[12,144,128]{2,1,0:T(8,128)(2,1)S(1)}, bf16[12,144,128]{2,1,0:T(8,128)(2,1)S(1)}, u32[]{:S(2)}, u32[]{:S(2)}) collective-permute-start(bf16[12,144,128]{2,1,0:T(8,128)(2,1)S(1)} %collective-permute-done.refs_7_), channel_id=1, source_target_pairs={{0,1},{1,0},{2,3},{3,2},{4,5},{5,4},{6,7},{7,6},{8,9},{9,8},{10,11... | collective-permute-start | bytes 1327112 | tf_op jit(solution)/shard_map/ppermute | solution.py:316
  62.1 2.5 %collective-permute-start.6 = (bf16[12,144,128]{2,1,0:T(8,128)(2,1)S(1)}, bf16[12,144,128]{2,1,0:T(8,128)(2,1)S(1)}, u32[]{:S(2)}, u32[]{:S(2)}) collective-permute-start(bf16[12,144,128]{2,1,0:T(8,128)(2,1)S(1)} %collective-permute-done.1.refs_9_), channel_id=1, source_target_pairs={{0,1},{1,0},{2,3},{3,2},{4,5},{5,4},{6,7},{7,6},{8,9},{9,8},{10,11... | collective-permute-start | bytes 1327112 | tf_op jit(solution)/shard_map/ppermute | solution.py:316
  62.3 2.4 %copy-start = (bf16[12,144,128]{2,1,0:T(8,128)(2,1)S(1)}, bf16[12,144,128]{2,1,0:T(8,128)(2,1)}, u32[]{:S(2)}) copy-start(bf16[12,144,128]{2,1,0:T(8,128)(2,1)} %get-tuple-element.38.refs_11_) | copy-start | bytes 1327108
  62.3 2.4 %copy-start.1 = (bf16[3,256,128]{2,1,0:T(8,128)(2,1)S(1)}, bf16[3,256,128]{2,1,0:T(8,128)(2,1)}, u32[]{:S(2)}) copy-start(bf16[3,256,128]{2,1,0:T(8,128)(2,1)} %constant.47.clone.refs_5_) | copy-start | bytes 589828
  62.3 2.4 %copy-start.2 = (bf16[3,128,256]{2,1,0:T(8,128)(2,1)S(1)}, bf16[3,128,256]{2,1,0:T(8,128)(2,1)}, u32[]{:S(2)}) copy-start(bf16[3,128,256]{2,1,0:T(8,128)(2,1)} %constant.46.clone.refs_4_) | copy-start | bytes 589828
  62.3 2.4 %copy-start.3 = (bf16[96,96]{1,0:T(8,128)(2,1)S(1)}, bf16[96,96]{1,0:T(8,128)(2,1)}, u32[]{:S(2)}) copy-start(bf16[96,96]{1,0:T(8,128)(2,1)} %constant.45.clone.refs_1_) | copy-start | bytes 55300
  62.3 2.4 %copy-start.4 = (bf16[96,96]{1,0:T(8,128)(2,1)S(1)}, bf16[96,96]{1,0:T(8,128)(2,1)}, u32[]{:S(2)}) copy-start(bf16[96,96]{1,0:T(8,128)(2,1)} %constant.44.clone.refs_0_) | copy-start | bytes 55300
  62.3 11.9 %collective-permute-start.10 = (bf16[12,144,128]{2,1,0:T(8,128)(2,1)S(1)}, bf16[12,144,128]{2,1,0:T(8,128)(2,1)S(1)}, u32[]{:S(2)}, u32[]{:S(2)}) collective-permute-start(bf16[12,144,128]{2,1,0:T(8,128)(2,1)S(1)} %slice_bitcast_fusion), channel_id=1, source_target_pairs={{0,1},{1,0},{2,3},{3,2},{4,5},{5,4},{6,7},{7,6},{8,9},{9,8},{10,11... | collective-permute-start | bytes 1327112 | tf_op jit(solution)/shard_map/ppermute | solution.py:316
  62.8 11.4 %collective-permute-start.9 = (bf16[12,144,128]{2,1,0:T(8,128)(2,1)S(1)}, bf16[12,144,128]{2,1,0:T(8,128)(2,1)S(1)}, u32[]{:S(2)}, u32[]{:S(2)}) collective-permute-start(bf16[12,144,128]{2,1,0:T(8,128)(2,1)S(1)} %slice_bitcast_fusion.1), channel_id=1, source_target_pairs={{0,1},{1,0},{2,3},{3,2},{4,5},{5,4},{6,7},{7,6},{8,9},{9,8},{10,11... | collective-permute-start | bytes 1327112 | tf_op jit(solution)/shard_map/ppermute | solution.py:316
  96.9 2.5 %collective-permute-start.11 = (bf16[2,12,144,128]{3,2,1,0:T(8,128)(2,1)S(1)}, bf16[2,12,144,128]{3,2,1,0:T(8,128)(2,1)S(1)}, u32[]{:S(2)}, u32[]{:S(2)}) collective-permute-start(bf16[2,12,144,128]{3,2,1,0:T(8,128)(2,1)S(1)} %get-tuple-element.44), channel_id=1, source_target_pairs={{0,1},{1,0},{2,3},{3,2},{4,5},{5,4},{6,7},{7,6},{8,9},{9,8},{10,11... | collective-permute-start | bytes 2654216 | tf_op jit(solution)/shard_map/ppermute | solution.py:316
  109.8 2.5 %collective-permute-start.12 = (bf16[2,12,144,128]{3,2,1,0:T(8,128)(2,1)S(1)}, bf16[2,12,144,128]{3,2,1,0:T(8,128)(2,1)S(1)}, u32[]{:S(2)}, u32[]{:S(2)}) collective-permute-start(bf16[2,12,144,128]{3,2,1,0:T(8,128)(2,1)S(1)} %get-tuple-element.50), channel_id=1, source_target_pairs={{0,1},{1,0},{2,3},{3,2},{4,5},{5,4},{6,7},{7,6},{8,9},{9,8},{10,11... | collective-permute-start | bytes 2654216 | tf_op jit(solution)/shard_map/ppermute | solution.py:316
  110.0 3.6 %collective-permute-start.15 = (bf16[2,12,144,128]{3,2,1,0:T(8,128)(2,1)S(1)}, bf16[2,12,144,128]{3,2,1,0:T(8,128)(2,1)S(1)}, u32[]{:S(2)}, u32[]{:S(2)}) collective-permute-start(bf16[2,12,144,128]{3,2,1,0:T(8,128)(2,1)S(1)} %get-tuple-element.53), channel_id=1, source_target_pairs={{0,1},{1,0},{2,3},{3,2},{4,5},{5,4},{6,7},{7,6},{8,9},{9,8},{10,11... | collective-permute-start | bytes 2654216 | tf_op jit(solution)/shard_map/ppermute | solution.py:316
  112.4 51.5 %copy-start.5 = (s32[2]{0:T(128)S(1)}, s32[2]{0:T(128)}, u32[]{:S(2)}) copy-start(s32[2]{0:T(128)} %pad_add_fusion.place) | copy-start | bytes 28
  112.4 46.3 %collective-permute-start.13 = (bf16[2,12,144,128]{3,2,1,0:T(8,128)(2,1)S(1)}, bf16[2,12,144,128]{3,2,1,0:T(8,128)(2,1)S(1)}, u32[]{:S(2)}, u32[]{:S(2)}) collective-permute-start(bf16[2,12,144,128]{3,2,1,0:T(8,128)(2,1)S(1)} %pad_maximum_fusion), channel_id=1, source_target_pairs={{0,4},{1,5},{2,6},{3,7},{4,8},{5,9},{6,10},{7,11},{8,12},{9,13},{1... | collective-permute-start | bytes 2654216 | tf_op jit(solution)/shard_map/ppermute | solution.py:316
  112.6 47.6 %collective-permute-start.14 = (bf16[2,12,144,128]{3,2,1,0:T(8,128)(2,1)S(1)}, bf16[2,12,144,128]{3,2,1,0:T(8,128)(2,1)S(1)}, u32[]{:S(2)}, u32[]{:S(2)}) collective-permute-start(bf16[2,12,144,128]{3,2,1,0:T(8,128)(2,1)S(1)} %pad_maximum_fusion.1), channel_id=1, source_target_pairs={{0,6},{1,7},{2,4},{3,5},{4,10},{5,11},{6,8},{7,9},{8,14},{9,15},{1... | collective-permute-start | bytes 2654216 | tf_op jit(solution)/shard_map/ppermute | solution.py:316
  113.7 50.2 %collective-permute-start.16 = (bf16[2,12,144,128]{3,2,1,0:T(8,128)(2,1)S(1)}, bf16[2,12,144,128]{3,2,1,0:T(8,128)(2,1)S(1)}, u32[]{:S(2)}, u32[]{:S(2)}) collective-permute-start(bf16[2,12,144,128]{3,2,1,0:T(8,128)(2,1)S(1)} %pad_maximum_fusion.2), channel_id=1, source_target_pairs={{0,2},{1,3},{2,0},{3,1},{4,6},{5,7},{6,4},{7,5},{8,10},{9,11},{10,... | collective-permute-start | bytes 2654216 | tf_op jit(solution)/shard_map/ppermute | solution.py:316
  113.9 22.4 %collective-permute-start.17 = (bf16[12,144,128]{2,1,0:T(8,128)(2,1)S(1)}, bf16[12,144,128]{2,1,0:T(8,128)(2,1)S(1)}, u32[]{:S(2)}, u32[]{:S(2)}) collective-permute-start(bf16[12,144,128]{2,1,0:T(8,128)(2,1)S(1)} %get-tuple-element.55), channel_id=1, source_target_pairs={{0,248},{1,249},{2,250},{3,251},{4,252},{5,253},{6,254},{7,255},{8... | collective-permute-start | bytes 1327112 | tf_op jit(solution)/shard_map/ppermute | solution.py:316
  123.5 35.2 %collective-permute-start.18 = (bf16[12,144,128]{2,1,0:T(8,128)(2,1)S(1)}, bf16[12,144,128]{2,1,0:T(8,128)(2,1)S(1)}, u32[]{:S(2)}, u32[]{:S(2)}) collective-permute-start(bf16[12,144,128]{2,1,0:T(8,128)(2,1)S(1)} %get-tuple-element.56), channel_id=1, source_target_pairs={{0,250},{1,251},{2,248},{3,249},{4,254},{5,255},{6,252},{7,253},{8... | collective-permute-start | bytes 1327112 | tf_op jit(solution)/shard_map/ppermute | solution.py:316
